TPU v7x, 512 devices: a whole 4x4x16 slice. The times are simulated.
512 devices in a mesh: uly: 8 (over x, y_hi), blk: 32 (over z, core), cfg: 2 (over y_lo).
Axes of the slice: x: 4, y: 4 (y_hi: 2, y_lo: 2; y = y_hi * 2 + y_lo), z: 16, core: 2. Of those that a mesh axis runs over, the one named last changes fastest.
Arguments:
- queries: bfloat16 [24576, 3072], P(('cfg', 'blk', 'uly')), parts along dimension 0, may hold values from -6 to 6
- key_vectors: bfloat16 [24576, 3072], P(('cfg', 'blk', 'uly')), parts along dimension 0, may hold values from -6 to 6
- value_vectors: bfloat16 [24576, 3072], P(('cfg', 'blk', 'uly')), parts along dimension 0, may hold values from -6 to 6
- windows: int32 [24, 3], replicated, may hold values from 1 to 3, as said below
Outputs:
- attended: bfloat16 [24576, 3072], P(('cfg', 'blk', 'uly')), parts along dimension 0
There are 2 independent parts, one for each index of `cfg`. A program takes and returns all parts, laid end to end along the dimension named above; an argument that names none is the same for every part. Nothing has to cross between parts.
Inputs may be any that keep to these rules, and one draw needn't show every extreme that they name: `windows`: column 0 is 3 for exactly two thirds of the heads and 1 for the others; columns 1 and 2 are each 3 for exactly half of the heads and 1 for the others.
All inputs are finite; a program needn't handle non-finite values.
Results may differ from a plain program's by a relative error of at most 0.0055.
Values may be sent and summed in bfloat16 or wider, within the bound.
No kernel may reach another device: no remote copies, remote signals or barrier semaphores. Data moves between devices by JAX's collectives and lax.ppermute only.
A program may use at most 64 MiB of HBM per device.

v0:
```python
import jax
import jax.numpy as jnp
from jax import lax
from jax.experimental import pallas as pl
from jax.experimental.pallas import tpu as pltpu
from jax.sharding import Mesh
from jax.sharding import PartitionSpec as P

HEADS = 24
DIM = 128
TILE = 384
PLACES = 16
USED = 12
WHOLE = 8
OWN, ONE, TWO, JOINED, PAIRED, FRAMES, LO, HI, HALVED, REST, FIRST, SECOND, HEAD = range(13)
MEMBERS = 2 * PLACES
CHUNK = 16
BATCH = 4
RUN = 8
PACK_VMEM = 62 * 1024 * 1024
GROUP = ("f", "g", "uly")
EXP2_SCALE = DIM**-0.5 * 1.4426950408889634
PARAMS = pltpu.CompilerParams(vmem_limit_bytes=20 * 1024 * 1024)


def is_open(win, axis, head):
    return win[axis, head] // 2


def fill_order(win, order, told=None):
    for place in range(2 * PLACES):
        order[place] = 0

    def put(head, carry):
        joined, apart = carry
        frames, heights, wide = (is_open(win, axis, head) for axis in range(3))
        both = wide * frames * heights
        place = jnp.where(both > 0, joined, USED - 1 - apart)
        place = jnp.where(wide > 0, place, head - joined - apart)
        order[(1 - wide) * PLACES + place] = head
        if told is not None:
            told(head, wide, place, frames, heights)
        return joined + both, apart + wide - both

    lax.fori_loop(0, HEADS, put, (jnp.int32(0), jnp.int32(0)))
    for place in range(WHOLE, USED):
        order[place + USED - WHOLE] = order[place]


def state_facts(columns, win, info, facts, order):
    place, row, column, frame = info[0], info[1], info[2], info[3]

    def count(head, joined):
        return joined + is_open(win, 0, head) * is_open(win, 1, head) * is_open(win, 2, head)

    split = jnp.where(lax.fori_loop(0, HEADS, count, jnp.int32(0)) <= WHOLE, 1, 0)

    def told(head, wide, at, frames, heights):
        half = jnp.where(frames > heights, row, frame)
        at = jnp.where(wide * split * at >= WHOLE, at + (USED - WHOLE) * half, at)
        facts[HEAD + head] = at // 8 * 16 + (1 - wide) * 8 + at % 8

    fill_order(win, order, told)
    head = order[row * PLACES + place]
    frames, heights = is_open(win, 0, head), is_open(win, 1, head)
    shared = jnp.where(place >= WHOLE, 1 - row, 0)
    halved = shared * split
    half = jnp.where(place >= USED, halved, 0)
    used = jnp.where((place < USED) | (halved > 0), 1, 0)
    wide = used * (1 - row)
    facts[OWN] = used
    lower = jnp.where(column > 0, wide, 0)
    upper = jnp.where(column < columns - 1, wide, 0)
    facts[ONE] = jnp.where(shared > 0, lower, upper)
    facts[TWO] = jnp.where(shared > 0, upper, lower)
    facts[JOINED] = frames * heights
    facts[PAIRED] = frames + heights - 2 * frames * heights
    facts[FRAMES] = frames
    facts[LO] = half
    facts[HI] = jnp.where(halved > 0, half + 1, 2)
    facts[HALVED] = shared
    facts[REST] = shared * (1 - split)
    by_row = halved * jnp.where(frames > heights, 1, 0)
    first = jnp.where(by_row > 0, half, 2 * half)
    facts[FIRST] = first
    facts[SECOND] = first + 1 + by_row


def pack(count, win_hbm, *refs):
    sources = refs[:count]
    out, win, held, staged, order, win_done, done, out_done = refs[-8:]
    first = pltpu.make_async_copy(win_hbm, win, win_done)
    first.start()
    copies = []
    for part, source in enumerate(sources):
        for chunk in range(source.shape[0] // CHUNK):
            rows = pl.ds(chunk * CHUNK, CHUNK)
            copy = pltpu.make_async_copy(
                source.at[rows, :], held.at[part, rows, :], done.at[part, chunk]
            )
            copy.start()
            copies.append(copy)
    first.wait()
    fill_order(win, order)
    for copy in copies:
        copy.wait()
    sent = []
    for member in range(MEMBERS):
        frame, row, uly = member // 16, member // 8 % 2, member % 8
        column = pl.multiple_of(order[row * PLACES + frame * 8 + uly] * DIM, DIM)
        for part in range(count):
            staged[member, :, part * DIM : (part + 1) * DIM] = held[part, :, pl.ds(column, DIM)]
        if member % BATCH == BATCH - 1:
            some = pl.ds(member + 1 - BATCH, BATCH)
            copy = pltpu.make_async_copy(
                staged.at[some], out.at[some], out_done.at[member // BATCH]
            )
            copy.start()
            sent.append(copy)
    for copy in sent:
        copy.wait()


def lanes(column, width):
    return jnp.broadcast_to(column, (column.shape[0], width))


def side_by_side(parts, axis):
    return parts[0] if len(parts) == 1 else jnp.concatenate(parts, axis=axis)


def score(query, kv, keys):
    parts = [
        lax.dot_general(
            query, kv[some, :DIM], (((1,), (1,)), ((), ())), preferred_element_type=jnp.float32
        )
        for some in keys
    ]
    return side_by_side(parts, 1)


def fold(scores, kv, keys, rows, before, write):
    copies = scores.shape[1] // DIM
    now = lanes(jnp.max(scores, axis=1, keepdims=True), DIM)
    if before:
        peak = before[0][rows, :]
        now = jnp.maximum(peak, now)
    weights = jnp.exp2((scores - jnp.concatenate([now] * copies, axis=1)) * EXP2_SCALE)
    values = side_by_side([kv[some, DIM : 2 * DIM] for some in keys], 0)
    with_ones = jnp.concatenate([values, jnp.ones_like(values)], axis=1)
    total = jnp.dot(weights.astype(jnp.bfloat16), with_ones, preferred_element_type=jnp.float32)
    if before:
        fade = jnp.exp2((peak - now) * EXP2_SCALE)
        total = before[1][rows, :] * jnp.concatenate([fade, fade], axis=1) + total
    write(rows, now, total)


def tile_rows(tile):
    return pl.ds(pl.multiple_of(tile * TILE, TILE), TILE)


def visit(query, kv, facts, before, write):
    def chains(blocks, keys):
        ahead = score(query[blocks[0], :], kv, keys[0])
        for index, rows in enumerate(blocks):
            scores = ahead
            if index + 1 < len(blocks):
                ahead = score(query[blocks[index + 1], :], kv, keys[index + 1])
            fold(scores, kv, keys[index], rows, before, write)

    @pl.when(facts[JOINED] > 0)
    def _():
        every = [pl.ds(0, 4 * TILE)]
        chains([pl.ds(512 * block, 512) for block in range(3)], [every] * 3)

    for index in range(2):
        here = (facts[LO] <= index) & (index < facts[HI])

        @pl.when(here & (facts[PAIRED] > 0))
        def _(index=index):
            low = jnp.where(facts[FRAMES] > 0, index, 2 * index)
            pair = [tile_rows(low), tile_rows(low + jnp.where(facts[FRAMES] > 0, 2, 1))]
            chains(pair, [pair, pair])

        @pl.when(here & (facts[JOINED] + facts[PAIRED] == 0))
        def _(index=index):
            tiles = [pl.ds(tile * TILE, TILE) for tile in (2 * index, 2 * index + 1)]
            chains(tiles, [[tile] for tile in tiles])


def keep(peak, total):
    def write(rows, now, sums):
        peak[rows, :] = now
        total[rows, :] = sums

    return write


def divided(total):
    return (total[:, :DIM] / total[:, DIM:]).astype(jnp.bfloat16)


def own_column(facts, qkv, peak, total):
    @pl.when(facts[OWN] > 0)
    def _():
        visit(qkv.at[:, 2 * DIM :], qkv, facts, None, keep(peak, total))


def cut(facts, qkv, half, rest):
    rest[...] = qkv[2 * TILE :, : 2 * DIM]
    half[:TILE, :] = qkv[tile_rows(facts[FIRST]), : 2 * DIM]
    half[TILE:, :] = qkv[tile_rows(facts[SECOND]), : 2 * DIM]


def put_together(facts, every, half, rest, kv, done):
    @pl.when(facts[HALVED] == 0)
    def _():
        kv[...] = every[...]

    @pl.when(facts[HALVED] > 0)
    def _():
        kv[tile_rows(facts[FIRST]), :] = half[:TILE, :]
        kv[tile_rows(facts[SECOND]), :] = half[TILE:, :]

    @pl.when(facts[REST] > 0)
    def _():
        copy = pltpu.make_async_copy(rest, kv.at[pl.ds(2 * TILE, 2 * TILE), :], done)
        copy.start()
        copy.wait()


def first_side(facts, qkv, every, half, peak_in, total_in, rest, peak, total, kv, done):
    @pl.when(facts[ONE] > 0)
    def _():
        put_together(facts, every, half, rest, kv, done)
        visit(qkv.at[:, 2 * DIM :], kv, facts, (peak_in, total_in), keep(peak, total))

    @pl.when(facts[OWN] > facts[ONE])
    def _():
        peak[...] = peak_in[...]
        total[...] = total_in[...]


def second_side(facts, qkv, every, half, peak_in, total_in, rest, out, kv, done):
    def write(rows, now, sums):
        out[rows, :] = divided(sums)

    @pl.when(facts[TWO] > 0)
    def _():
        put_together(facts, every, half, rest, kv, done)
        visit(qkv.at[:, 2 * DIM :], kv, facts, (peak_in, total_in), write)

    @pl.when(facts[OWN] > facts[TWO])
    def _():
        out[...] = divided(total_in[...])


def unpack(facts, received, out, staged, done):
    copies = []
    for head in range(HEADS):
        staged[:, head * DIM : (head + 1) * DIM] = received[facts[HEAD + head]]
        if head % RUN == RUN - 1:
            columns = pl.ds((head + 1 - RUN) * DIM, RUN * DIM)
            copy = pltpu.make_async_copy(
                staged.at[:, columns], out.at[:, columns], done.at[head // RUN]
            )
            copy.start()
            copies.append(copy)
    for copy in copies:
        copy.wait()


HBM = pl.BlockSpec(memory_space=pltpu.HBM)
SMEM = pl.BlockSpec(memory_space=pltpu.SMEM)
VMEM = pl.BlockSpec(memory_space=pltpu.VMEM)
ORDER = pltpu.SMEM((MEMBERS,), jnp.int32)


def call(kernel, shapes, operands, far=(), scratch=()):
    return pl.pallas_call(
        kernel,
        out_shape=shapes,
        in_specs=[SMEM] + [VMEM] * (len(operands) - 1) + [HBM] * len(far),
        out_specs=jax.tree.map(lambda _: VMEM, shapes),
        scratch_shapes=list(scratch),
        compiler_params=PARAMS,
    )(*operands, *far)


def shards(queries, key_vectors, value_vectors, windows):
    tokens, width = queries.shape
    rows = MEMBERS * tokens
    columns = lax.axis_size("col")
    bf16, f32 = jnp.bfloat16, jnp.float32
    place = lax.axis_index("f") * 8 + lax.axis_index("uly")
    info = jnp.stack(
        [place, lax.axis_index("g"), lax.axis_index("col"), lax.axis_index("f")]
    ).astype(jnp.int32)
    win = windows.T
    sources = [key_vectors, value_vectors, queries]
    count = len(sources)

    def pack_kernel(*refs):
        pack(count, *refs)

    def exchange(value):
        return lax.all_to_all(value, GROUP, split_axis=0, concat_axis=0, tiled=True)

    sendable = pl.pallas_call(
        pack_kernel,
        out_shape=jax.ShapeDtypeStruct((MEMBERS, tokens, count * DIM), bf16),
        in_specs=[HBM] * (1 + count),
        out_specs=HBM,
        scratch_shapes=[
            pltpu.SMEM(win.shape, jnp.int32),
            pltpu.VMEM((count, tokens, width), bf16),
            pltpu.VMEM((MEMBERS, tokens, count * DIM), bf16),
            ORDER,
            pltpu.SemaphoreType.DMA,
            pltpu.SemaphoreType.DMA((count, tokens // CHUNK)),
            pltpu.SemaphoreType.DMA((MEMBERS // BATCH,)),
        ],
        compiler_params=pltpu.CompilerParams(vmem_limit_bytes=PACK_VMEM),
    )(win, *sources)
    qkv = exchange(sendable)
    def facts_kernel(*refs):
        state_facts(columns, *refs)

    facts = pl.pallas_call(
        facts_kernel,
        out_shape=jax.ShapeDtypeStruct((HEAD + HEADS,), jnp.int32),
        in_specs=[SMEM, SMEM],
        out_specs=SMEM,
        scratch_shapes=[ORDER],
        compiler_params=PARAMS,
    )(win, info)

    whole = jnp.sum(jnp.prod(windows // 2, axis=1)) > WHOLE
    qkv, facts, whole = lax.optimization_barrier((qkv, facts, whole))
    qkv = qkv.reshape(rows, count * DIM)

    def beside(value, frame):
        up = [
            (((uly * columns + col) * 2 + frame) * 2, ((uly * columns + col + 1) * 2 + frame) * 2)
            for uly in range(8)
            for col in range(columns - 1)
        ]
        along = ("uly", "col", "f", "g")
        return lax.ppermute(value, along, up), lax.ppermute(value, along, [(b, a) for a, b in up])

    lower, upper = beside(qkv[:, : 2 * DIM], 0)
    pair = jax.ShapeDtypeStruct((rows // 2, 2 * DIM), bf16)
    half, rest = call(cut, (pair, pair), [facts, qkv])
    low_half, up_half = beside(half, 1)

    column = lax.axis_index("col")

    def send_rest(rest):
        near = jnp.abs(jnp.arange(columns) - column) == 1
        sent = jnp.where(near[:, None, None], rest[None], jnp.zeros_like(rest)[None])
        got = lax.all_to_all(sent, "col", split_axis=0, concat_axis=0, tiled=True)
        return tuple(
            lax.dynamic_index_in_dim(got, jnp.clip(at, 0, columns - 1), 0, keepdims=False)
            for at in (column - 1, column + 1)
        )

    def no_rest(rest):
        return (jnp.zeros_like(rest),) * 2

    low_rest, up_rest = lax.cond(whole, send_rest, no_rest, rest)

    state = (jax.ShapeDtypeStruct((rows, DIM), f32), jax.ShapeDtypeStruct((rows, 2 * DIM), f32))

    def own_kernel(facts, qkv, low_rest, up_rest, peak, total):
        del low_rest, up_rest
        own_column(facts, qkv, peak, total)

    peak, total = call(own_kernel, state, [facts, qkv], [low_rest, up_rest])
    joined = [pltpu.VMEM((rows, 2 * DIM), bf16), pltpu.SemaphoreType.DMA]
    peak, total = call(
        first_side, state, [facts, qkv, upper, low_half, peak, total], [low_rest], joined
    )
    result = call(
        second_side,
        jax.ShapeDtypeStruct((rows, DIM), bf16),
        [facts, qkv, lower, up_half, peak, total],
        [up_rest],
        joined,
    )
    back = exchange(result.reshape(MEMBERS, tokens, DIM))
    return pl.pallas_call(
        unpack,
        out_shape=jax.ShapeDtypeStruct((tokens, width), bf16),
        in_specs=[SMEM, VMEM],
        out_specs=HBM,
        scratch_shapes=[
            pltpu.VMEM((tokens, width), bf16),
            pltpu.SemaphoreType.DMA((HEADS // RUN,)),
        ],
        compiler_params=PARAMS,
    )(facts, back)


def solution(mesh):
    uly, blk, cfg = (mesh.shape[name] for name in ("uly", "blk", "cfg"))
    fine = Mesh(mesh.devices.reshape(uly, blk // 4, 2, 2, cfg), ("uly", "col", "f", "g", "cfg"))
    tokens = P(("cfg", "col", "f", "g", "uly"), None)
    return jax.shard_map(
        shards,
        mesh=fine,
        in_specs=(tokens, tokens, tokens, P()),
        out_specs=tokens,
        check_vma=False,
    )
```

profile of v0, /device:TPU:353, one launch (start us, length us, event | category | flops | bytes accessed | tf_op | source)
XLA Modules:
  0.0 74.6 jit_solution(1979475920295079317)
XLA Ops:
  0.0 0.0 copy-start
  0.0 2.7 %shard_map.46 = bf16[32,48,384]{2,1,0:T(8,128)(2,1)} custom-call(s32[3,24]{1,0:T(4,128)} %bitcast.17, bf16[48,3072]{1,0:T(8,128)(2,1)} %refs_1_.1, bf16[48,3072]{1,0:T(8,128)(2,1)} %refs_2_.1, bf16[48,3072]{1,0:T(8,128)(2,1)} %refs_3_.1), custom_call_target="tpu_custom_call" | custom-call | tf_op jit(solution)/shard_map/pallas_call | solution.py:309
  2.8 8.9 %all-to-all-start.1 = ((bf16[32,48,384]{2,1,0:T(8,128)(2,1)}), bf16[32,48,384]{2,1,0:T(8,128)(2,1)S(1)}, u32[]{:S(2)}, u32[]{:S(2)}) async-start(bf16[32,48,384]{2,1,0:T(8,128)(2,1)} %shard_map.46), calls=%async_computation.1 | async-start | bytes 2359296 | tf_op jit(solution)/shard_map/all_to_all | solution.py:307
  11.7 0.1 pad_add_fusion.refs_1_
  11.8 0.0 copy-done
  11.8 2.5 %shard_map.47.facts = s32[36]{0:T(128)S(1)} custom-call(s32[3,24]{1,0:T(4,128)S(1)} %bitcast.18, s32[4]{0:T(128)S(1)} %pad_add_fusion.refs_1_), custom_call_target="tpu_custom_call" | custom-call | tf_op jit(solution)/shard_map/pallas_call | solution.py:329
  14.3 0.6 reduce_sum.9
  15.6 14.8 %all-to-all-done.1 = bf16[32,48,384]{2,1,0:T(8,128)(2,1)S(1)} async-done(((bf16[32,48,384]{2,1,0:T(8,128)(2,1)}), bf16[32,48,384]{2,1,0:T(8,128)(2,1)S(1)}, u32[]{:S(2)}, u32[]{:S(2)}) %all-to-all-start.1) | async-done | bytes 1179680 | tf_op jit(solution)/shard_map/all_to_all | solution.py:307
  30.4 0.9 %slice.4 = bf16[1536,256]{1,0:T(8,128)(2,1)} slice(bf16[1536,384]{1,0:T(8,128)(2,1)S(1)} %bitcast.11), slice={[0:1536], [0:256]} | slice | bytes 1572864 | tf_op jit(solution)/shard_map/slice | solution.py:351
  31.4 0.7 collective-permute-start.2
  32.1 0.7 collective-permute-start
  32.8 1.5 %shard_map.48 = (bf16[768,256]{1,0:T(8,128)(2,1)}, bf16[768,256]{1,0:T(8,128)(2,1)}) custom-call(s32[36]{0:T(128)S(1)} %shard_map.47.facts, bf16[1536,384]{1,0:T(8,128)(2,1)S(1)} %bitcast.12), custom_call_target="tpu_custom_call" | custom-call | tf_op jit(solution)/shard_map/pallas_call | solution.py:280
  34.3 0.7 collective-permute-start.3
  35.0 0.7 collective-permute-start.1
  35.7 1.6 %conditional.1 = (bf16[768,256]{1,0:T(8,128)(2,1)}, bf16[768,256]{1,0:T(8,128)(2,1)}) conditional(s32[]{:T(128)} %convert_element_type.3, () %tuple.15, (s32[]{:T(128)}, bf16[768,256]{1,0:T(8,128)(2,1)}) %tuple.16), branch_computations={%region_2.3_spmd, %region_3.4_spmd} | conditional | flops 1572894 | bytes 14549140 | solution.py:370
  35.7 0.8 %broadcast.24 = bf16[768,256]{1,0:T(8,128)(2,1)} broadcast(bf16[]{:T(256)} %constant.41.clone), dimensions={} | broadcast | bytes 393218 | tf_op jit(solution)/shard_map/broadcast.1
  36.4 0.8 %broadcast.24.clone = bf16[768,256]{1,0:T(8,128)(2,1)} broadcast(bf16[]{:T(256)} %constant.41.clone), dimensions={} | broadcast | bytes 393218 | tf_op jit(solution)/shard_map/broadcast.1
  37.2 2.7 %shard_map.49 = (f32[1536,128]{1,0:T(8,128)S(1)}, f32[1536,256]{1,0:T(8,128)S(1)}) custom-call(s32[36]{0:T(128)S(1)} %shard_map.47.facts, bf16[1536,384]{1,0:T(8,128)(2,1)S(1)} %bitcast.13, bf16[768,256]{1,0:T(8,128)(2,1)} %get-tuple-element.27.low_rest.rest, bf16[768,256]{1,0:T(8,128)(2,1)} %get-tuple-element.28.up_rest.rest), custom_call_target="tpu_custom_call" | custom-call | tf_op jit(solution)/shard_map/pallas_call | solution.py:280
  39.9 0.0 collective-permute-done.3.half
  39.9 0.0 collective-permute-done.2.every
  40.0 0.9 %shard_map.50 = (f32[1536,128]{1,0:T(8,128)S(1)}, f32[1536,256]{1,0:T(8,128)S(1)}) custom-call(s32[36]{0:T(128)S(1)} %shard_map.47.facts, bf16[1536,384]{1,0:T(8,128)(2,1)S(1)} %bitcast.14, bf16[1536,256]{1,0:T(8,128)(2,1)S(1)} %collective-permute-done.2.every, bf16[768,256]{1,0:T(8,128)(2,1)S(1)} %collective-permute-done.3.half, ...), custom_call_target="tpu_custom_call" | custom-call | tf_op jit(solution)/shard_map/pallas_call | solution.py:280
  40.9 0.0 collective-permute-done.1.half
  40.9 0.0 collective-permute-done.every
  40.9 0.7 shard_map.51
  41.6 31.5 %all_to_all.14.received = bf16[32,48,128]{2,1,0:T(8,128)(2,1)S(1)} all-to-all(bf16[32,48,128]{2,1,0:T(8,128)(2,1)S(1)} %bitcast.16), channel_id=1, replica_groups=mesh['uly'=8,'col'=8,'f'=2,'g'=2,'cfg'=2] {'f','g','uly'}, dimensions={0} | all-to-all | bytes 786432 | tf_op jit(solution)/shard_map/all_to_all | solution.py:307
  73.1 1.3 %shard_map.52 = bf16[48,3072]{1,0:T(8,128)(2,1)} custom-call(s32[36]{0:T(128)S(1)} %shard_map.47.facts, bf16[32,48,128]{2,1,0:T(8,128)(2,1)S(1)} %all_to_all.14.received), custom_call_target="tpu_custom_call" | custom-call | tf_op jit(solution)/shard_map/pallas_call | solution.py:391
  (1 shorter events, 0.0 us)
Async XLA Ops:
  0.0 11.8 %copy-start = (s32[24,3]{0,1:T(4,128)S(1)}, s32[24,3]{0,1:T(4,128)}, u32[]{:S(2)}) copy-start(s32[24,3]{0,1:T(4,128)} %param.9) | copy-start | bytes 868
  2.8 27.7 %all-to-all-start.1 = ((bf16[32,48,384]{2,1,0:T(8,128)(2,1)}), bf16[32,48,384]{2,1,0:T(8,128)(2,1)S(1)}, u32[]{:S(2)}, u32[]{:S(2)}) async-start(bf16[32,48,384]{2,1,0:T(8,128)(2,1)} %shard_map.46), calls=%async_computation.1 | async-start | bytes 2359296 | tf_op jit(solution)/shard_map/all_to_all | solution.py:307
  31.4 8.6 %collective-permute-start.2 = (bf16[1536,256]{1,0:T(8,128)(2,1)}, bf16[1536,256]{1,0:T(8,128)(2,1)S(1)}, u32[]{:S(2)}, u32[]{:S(2)}) collective-permute-start(bf16[1536,256]{1,0:T(8,128)(2,1)} %slice.4), channel_id=1, source_target_pairs={{8,0},{16,8},{24,16},{32,24},{40,32},{48,40},{56,48},{72,64},{80,7... | collective-permute-start | bytes 2359304 | tf_op jit(solution)/shard_map/ppermute | solution.py:349
  32.1 8.8 %collective-permute-start = (bf16[1536,256]{1,0:T(8,128)(2,1)}, bf16[1536,256]{1,0:T(8,128)(2,1)S(1)}, u32[]{:S(2)}, u32[]{:S(2)}) collective-permute-start(bf16[1536,256]{1,0:T(8,128)(2,1)} %slice.4), channel_id=1, source_target_pairs={{0,8},{8,16},{16,24},{24,32},{32,40},{40,48},{48,56},{64,72},{72,8... | collective-permute-start | bytes 2359304 | tf_op jit(solution)/shard_map/ppermute | solution.py:349
  34.3 5.6 %collective-permute-start.3 = (bf16[768,256]{1,0:T(8,128)(2,1)}, bf16[768,256]{1,0:T(8,128)(2,1)S(1)}, u32[]{:S(2)}, u32[]{:S(2)}) collective-permute-start(bf16[768,256]{1,0:T(8,128)(2,1)} %get-tuple-element.24), channel_id=1, source_target_pairs={{4,12},{12,20},{20,28},{28,36},{36,44},{44,52},{52,60},{68,76},{76... | collective-permute-start | bytes 1179656 | tf_op jit(solution)/shard_map/ppermute | solution.py:349
  35.0 5.9 %collective-permute-start.1 = (bf16[768,256]{1,0:T(8,128)(2,1)}, bf16[768,256]{1,0:T(8,128)(2,1)S(1)}, u32[]{:S(2)}, u32[]{:S(2)}) collective-permute-start(bf16[768,256]{1,0:T(8,128)(2,1)} %get-tuple-element.24), channel_id=1, source_target_pairs={{12,4},{20,12},{28,20},{36,28},{44,36},{52,44},{60,52},{76,68},{84... | collective-permute-start | bytes 1179656 | tf_op jit(solution)/shard_map/ppermute | solution.py:349
where the time goes:
time: 75 us; the launch traced here: 74.6 us
  blocking collectives  31.5 us (42%)
  waiting for transfers between devices  14.8 us (20%)
  Pallas kernels  12.4 us (17%)
  starting transfers between devices  11.7 us (16%)
  local copies, waits for them, and re-layouts  2.49 us (3%)
  between operations  0.96 us (1%)
    all_to_all x1, blocking collectives, exchange(): return lax.all_to_all(value, GROUP, split_axis=0, concat_axis=0, tiled=True)  31.5 us
    all_to_all x1, waiting for transfers between devices, exchange(): return lax.all_to_all(value, GROUP, split_axis=0, concat_axis=0, tiled=True)  14.8 us
    all_to_all x1, starting transfers between devices, exchange(): return lax.all_to_all(value, GROUP, split_axis=0, concat_axis=0, tiled=True)  8.9 us
    pallas_call x4, Pallas kernels, call(): pl.pallas_call(kernel, out_shape=shapes, in_specs=[SMEM] + [VMEM] * (len(...  5.81 us
    pallas_call x1, Pallas kernels, shards(): pl.pallas_call(pack_kernel, out_shape=jax.ShapeDtypeStruct((MEMBERS, toke...  2.75 us
    pallas_call x1, Pallas kernels, shards(): pl.pallas_call(facts_kernel, out_shape=jax.ShapeDtypeStruct((HEAD + HEADS...  2.51 us
    another operation x2, local copies, waits for them, and re-layouts  1.54 us
  transfers between devices with their start and end apart: 5, of which 1 were waited for; matrix products, arithmetic and copies ran while one was open for 3% of the time, Pallas kernels for 10%

commit v1 on v0

--- a/solution.py
+++ b/solution.py
@@ -15,7 +15,7 @@
 OWN, ONE, TWO, JOINED, PAIRED, FRAMES, LO, HI, HALVED, REST, FIRST, SECOND, HEAD = range(13)
 MEMBERS = 2 * PLACES
 CHUNK = 16
-BATCH = 4
+BATCH = 16
 RUN = 8
 PACK_VMEM = 62 * 1024 * 1024
 GROUP = ("f", "g", "uly")
@@ -99,24 +99,28 @@
                 source.at[rows, :], held.at[part, rows, :], done.at[part, chunk]
             )
             copy.start()
-            copies.append(copy)
+            copies.append((part, copy))
     first.wait()
     fill_order(win, order)
-    for copy in copies:
-        copy.wait()
     sent = []
-    for member in range(MEMBERS):
-        frame, row, uly = member // 16, member // 8 % 2, member % 8
-        column = pl.multiple_of(order[row * PLACES + frame * 8 + uly] * DIM, DIM)
-        for part in range(count):
+    for part in range(count):
+        for index, copy in copies:
+            if index == part:
+                copy.wait()
+        column_range = pl.ds(part * DIM, DIM)
+        for member in range(MEMBERS):
+            frame, row, uly = member // 16, member // 8 % 2, member % 8
+            column = pl.multiple_of(order[row * PLACES + frame * 8 + uly] * DIM, DIM)
             staged[member, :, part * DIM : (part + 1) * DIM] = held[part, :, pl.ds(column, DIM)]
-        if member % BATCH == BATCH - 1:
-            some = pl.ds(member + 1 - BATCH, BATCH)
-            copy = pltpu.make_async_copy(
-                staged.at[some], out.at[some], out_done.at[member // BATCH]
-            )
-            copy.start()
-            sent.append(copy)
+            if member % BATCH == BATCH - 1:
+                some = pl.ds(member + 1 - BATCH, BATCH)
+                copy = pltpu.make_async_copy(
+                    staged.at[some, :, column_range],
+                    out.at[some, :, column_range],
+                    out_done.at[part, member // BATCH],
+                )
+                copy.start()
+                sent.append(copy)
     for copy in sent:
         copy.wait()
 
@@ -318,7 +322,7 @@
             ORDER,
             pltpu.SemaphoreType.DMA,
             pltpu.SemaphoreType.DMA((count, tokens // CHUNK)),
-            pltpu.SemaphoreType.DMA((MEMBERS // BATCH,)),
+            pltpu.SemaphoreType.DMA((count, MEMBERS // BATCH)),
         ],
         compiler_params=pltpu.CompilerParams(vmem_limit_bytes=PACK_VMEM),
     )(win, *sources)

time: 75 us -> 75.2 us (level)
  the two profiles are of different devices: /device:TPU:353 before, /device:TPU:417 now
where the time goes in v1:
time: 75.2 us; the launch traced here: 74.9 us
  blocking collectives  31.1 us (41%)
  waiting for transfers between devices  14.8 us (20%)
  Pallas kernels  13.1 us (17%)
  starting transfers between devices  11.7 us (16%)
  local copies, waits for them, and re-layouts  2.49 us (3%)
  between operations  0.96 us (1%)
    all_to_all x1, blocking collectives, exchange(): return lax.all_to_all(value, GROUP, split_axis=0, concat_axis=0, tiled=True)  31.1 us
    all_to_all x1, waiting for transfers between devices, exchange(): return lax.all_to_all(value, GROUP, split_axis=0, concat_axis=0, tiled=True)  14.8 us
    all_to_all x1, starting transfers between devices, exchange(): return lax.all_to_all(value, GROUP, split_axis=0, concat_axis=0, tiled=True)  8.9 us
    pallas_call x4, Pallas kernels, call(): pl.pallas_call(kernel, out_shape=shapes, in_specs=[SMEM] + [VMEM] * (len(...  6.55 us
    pallas_call x1, Pallas kernels, shards(): pl.pallas_call(pack_kernel, out_shape=jax.ShapeDtypeStruct((MEMBERS, toke...  2.75 us
    pallas_call x1, Pallas kernels, shards(): pl.pallas_call(facts_kernel, out_shape=jax.ShapeDtypeStruct((HEAD + HEADS...  2.51 us
    another operation x2, local copies, waits for them, and re-layouts  1.54 us
  transfers between devices with their start and end apart: 5, of which 1 were waited for; matrix products, arithmetic and copies ran while one was open for 3% of the time, Pallas kernels for 11%

profile of v1, /device:TPU:417, one launch (start us, length us, event | category | flops | bytes accessed | tf_op | source)
XLA Modules:
  0.0 74.9 jit_solution(2546952623375795061)
XLA Ops:
  0.0 0.0 copy-start
  0.0 2.8 %shard_map.46 = bf16[32,48,384]{2,1,0:T(8,128)(2,1)} custom-call(s32[3,24]{1,0:T(4,128)} %bitcast.17, bf16[48,3072]{1,0:T(8,128)(2,1)} %refs_1_.1, bf16[48,3072]{1,0:T(8,128)(2,1)} %refs_2_.1, bf16[48,3072]{1,0:T(8,128)(2,1)} %refs_3_.1), custom_call_target="tpu_custom_call" | custom-call | tf_op jit(solution)/shard_map/pallas_call | solution.py:313
  2.8 8.9 %all-to-all-start.1 = ((bf16[32,48,384]{2,1,0:T(8,128)(2,1)}), bf16[32,48,384]{2,1,0:T(8,128)(2,1)S(1)}, u32[]{:S(2)}, u32[]{:S(2)}) async-start(bf16[32,48,384]{2,1,0:T(8,128)(2,1)} %shard_map.46), calls=%async_computation.1 | async-start | bytes 2359296 | tf_op jit(solution)/shard_map/all_to_all | solution.py:311
  11.7 0.1 pad_add_fusion.refs_1_
  11.8 0.0 copy-done
  11.8 2.5 %shard_map.47.facts = s32[36]{0:T(128)S(1)} custom-call(s32[3,24]{1,0:T(4,128)S(1)} %bitcast.18, s32[4]{0:T(128)S(1)} %pad_add_fusion.refs_1_), custom_call_target="tpu_custom_call" | custom-call | tf_op jit(solution)/shard_map/pallas_call | solution.py:333
  14.3 0.6 reduce_sum.9
  15.6 14.8 %all-to-all-done.1 = bf16[32,48,384]{2,1,0:T(8,128)(2,1)S(1)} async-done(((bf16[32,48,384]{2,1,0:T(8,128)(2,1)}), bf16[32,48,384]{2,1,0:T(8,128)(2,1)S(1)}, u32[]{:S(2)}, u32[]{:S(2)}) %all-to-all-start.1) | async-done | bytes 1179680 | tf_op jit(solution)/shard_map/all_to_all | solution.py:311
  30.4 0.9 %slice.4 = bf16[1536,256]{1,0:T(8,128)(2,1)} slice(bf16[1536,384]{1,0:T(8,128)(2,1)S(1)} %bitcast.11), slice={[0:1536], [0:256]} | slice | bytes 1572864 | tf_op jit(solution)/shard_map/slice | solution.py:355
  31.4 0.7 collective-permute-start.2
  32.1 0.7 collective-permute-start
  32.8 1.5 %shard_map.48 = (bf16[768,256]{1,0:T(8,128)(2,1)}, bf16[768,256]{1,0:T(8,128)(2,1)}) custom-call(s32[36]{0:T(128)S(1)} %shard_map.47.facts, bf16[1536,384]{1,0:T(8,128)(2,1)S(1)} %bitcast.12), custom_call_target="tpu_custom_call" | custom-call | tf_op jit(solution)/shard_map/pallas_call | solution.py:284
  34.3 0.7 collective-permute-start.3
  35.0 0.7 collective-permute-start.1
  35.7 1.6 %conditional.1 = (bf16[768,256]{1,0:T(8,128)(2,1)}, bf16[768,256]{1,0:T(8,128)(2,1)}) conditional(s32[]{:T(128)} %convert_element_type.3, () %tuple.15, (s32[]{:T(128)}, bf16[768,256]{1,0:T(8,128)(2,1)}) %tuple.16), branch_computations={%region_2.3_spmd, %region_3.4_spmd} | conditional | flops 1572894 | bytes 14549140 | solution.py:374
  35.7 0.8 %broadcast.24 = bf16[768,256]{1,0:T(8,128)(2,1)} broadcast(bf16[]{:T(256)} %constant.41.clone), dimensions={} | broadcast | bytes 393218 | tf_op jit(solution)/shard_map/broadcast.1
  36.5 0.8 %broadcast.24.clone = bf16[768,256]{1,0:T(8,128)(2,1)} broadcast(bf16[]{:T(256)} %constant.41.clone), dimensions={} | broadcast | bytes 393218 | tf_op jit(solution)/shard_map/broadcast.1
  37.2 3.4 %shard_map.49 = (f32[1536,128]{1,0:T(8,128)S(1)}, f32[1536,256]{1,0:T(8,128)S(1)}) custom-call(s32[36]{0:T(128)S(1)} %shard_map.47.facts, bf16[1536,384]{1,0:T(8,128)(2,1)S(1)} %bitcast.13, bf16[768,256]{1,0:T(8,128)(2,1)} %get-tuple-element.27.low_rest.rest, bf16[768,256]{1,0:T(8,128)(2,1)} %get-tuple-element.28.up_rest.rest), custom_call_target="tpu_custom_call" | custom-call | tf_op jit(solution)/shard_map/pallas_call | solution.py:284
  40.7 0.0 collective-permute-done.3.half
  40.7 0.0 collective-permute-done.2.every
  40.7 0.9 %shard_map.50 = (f32[1536,128]{1,0:T(8,128)S(1)}, f32[1536,256]{1,0:T(8,128)S(1)}) custom-call(s32[36]{0:T(128)S(1)} %shard_map.47.facts, bf16[1536,384]{1,0:T(8,128)(2,1)S(1)} %bitcast.14, bf16[1536,256]{1,0:T(8,128)(2,1)S(1)} %collective-permute-done.2.every, bf16[768,256]{1,0:T(8,128)(2,1)S(1)} %collective-permute-done.3.half, ...), custom_call_target="tpu_custom_call" | custom-call | tf_op jit(solution)/shard_map/pallas_call | solution.py:284
  41.6 0.0 collective-permute-done.1.half
  41.6 0.0 collective-permute-done.every
  41.7 0.7 shard_map.51
  42.3 31.1 %all_to_all.14.received = bf16[32,48,128]{2,1,0:T(8,128)(2,1)S(1)} all-to-all(bf16[32,48,128]{2,1,0:T(8,128)(2,1)S(1)} %bitcast.16), channel_id=1, replica_groups=mesh['uly'=8,'col'=8,'f'=2,'g'=2,'cfg'=2] {'f','g','uly'}, dimensions={0} | all-to-all | bytes 786432 | tf_op jit(solution)/shard_map/all_to_all | solution.py:311
  73.4 1.3 %shard_map.52 = bf16[48,3072]{1,0:T(8,128)(2,1)} custom-call(s32[36]{0:T(128)S(1)} %shard_map.47.facts, bf16[32,48,128]{2,1,0:T(8,128)(2,1)S(1)} %all_to_all.14.received), custom_call_target="tpu_custom_call" | custom-call | tf_op jit(solution)/shard_map/pallas_call | solution.py:395
  (1 shorter events, 0.0 us)
Async XLA Ops:
  0.0 11.8 %copy-start = (s32[24,3]{0,1:T(4,128)S(1)}, s32[24,3]{0,1:T(4,128)}, u32[]{:S(2)}) copy-start(s32[24,3]{0,1:T(4,128)} %param.9) | copy-start | bytes 868
  2.8 27.7 %all-to-all-start.1 = ((bf16[32,48,384]{2,1,0:T(8,128)(2,1)}), bf16[32,48,384]{2,1,0:T(8,128)(2,1)S(1)}, u32[]{:S(2)}, u32[]{:S(2)}) async-start(bf16[32,48,384]{2,1,0:T(8,128)(2,1)} %shard_map.46), calls=%async_computation.1 | async-start | bytes 2359296 | tf_op jit(solution)/shard_map/all_to_all | solution.py:311
  31.4 9.3 %collective-permute-start.2 = (bf16[1536,256]{1,0:T(8,128)(2,1)}, bf16[1536,256]{1,0:T(8,128)(2,1)S(1)}, u32[]{:S(2)}, u32[]{:S(2)}) collective-permute-start(bf16[1536,256]{1,0:T(8,128)(2,1)} %slice.4), channel_id=1, source_target_pairs={{8,0},{16,8},{24,16},{32,24},{40,32},{48,40},{56,48},{72,64},{80,7... | collective-permute-start | bytes 2359304 | tf_op jit(solution)/shard_map/ppermute | solution.py:353
  32.1 9.6 %collective-permute-start = (bf16[1536,256]{1,0:T(8,128)(2,1)}, bf16[1536,256]{1,0:T(8,128)(2,1)S(1)}, u32[]{:S(2)}, u32[]{:S(2)}) collective-permute-start(bf16[1536,256]{1,0:T(8,128)(2,1)} %slice.4), channel_id=1, source_target_pairs={{0,8},{8,16},{16,24},{24,32},{32,40},{40,48},{48,56},{64,72},{72,8... | collective-permute-start | bytes 2359304 | tf_op jit(solution)/shard_map/ppermute | solution.py:353
  34.3 6.4 %collective-permute-start.3 = (bf16[768,256]{1,0:T(8,128)(2,1)}, bf16[768,256]{1,0:T(8,128)(2,1)S(1)}, u32[]{:S(2)}, u32[]{:S(2)}) collective-permute-start(bf16[768,256]{1,0:T(8,128)(2,1)} %get-tuple-element.24), channel_id=1, source_target_pairs={{4,12},{12,20},{20,28},{28,36},{36,44},{44,52},{52,60},{68,76},{76... | collective-permute-start | bytes 1179656 | tf_op jit(solution)/shard_map/ppermute | solution.py:353
  35.0 6.7 %collective-permute-start.1 = (bf16[768,256]{1,0:T(8,128)(2,1)}, bf16[768,256]{1,0:T(8,128)(2,1)S(1)}, u32[]{:S(2)}, u32[]{:S(2)}) collective-permute-start(bf16[768,256]{1,0:T(8,128)(2,1)} %get-tuple-element.24), channel_id=1, source_target_pairs={{12,4},{20,12},{28,20},{36,28},{44,36},{52,44},{60,52},{76,68},{84... | collective-permute-start | bytes 1179656 | tf_op jit(solution)/shard_map/ppermute | solution.py:353

commit v2 on v1

--- a/solution.py
+++ b/solution.py
@@ -24,15 +24,14 @@
 
 
 def is_open(win, axis, head):
-    return win[axis, head] // 2
+    return win[axis, head] >> 1
 
 
 def fill_order(win, order, told=None):
-    for place in range(2 * PLACES):
+    for place in range(PLACES + USED, 2 * PLACES):
         order[place] = 0
-
-    def put(head, carry):
-        joined, apart = carry
+    joined, apart = jnp.int32(0), jnp.int32(0)
+    for head in range(HEADS):
         frames, heights, wide = (is_open(win, axis, head) for axis in range(3))
         both = wide * frames * heights
         place = jnp.where(both > 0, joined, USED - 1 - apart)
@@ -40,9 +39,7 @@
         order[(1 - wide) * PLACES + place] = head
         if told is not None:
             told(head, wide, place, frames, heights)
-        return joined + both, apart + wide - both
-
-    lax.fori_loop(0, HEADS, put, (jnp.int32(0), jnp.int32(0)))
+        joined, apart = joined + both, apart + wide - both
     for place in range(WHOLE, USED):
         order[place + USED - WHOLE] = order[place]
 
@@ -50,10 +47,10 @@
 def state_facts(columns, win, info, facts, order):
     place, row, column, frame = info[0], info[1], info[2], info[3]
 
-    def count(head, joined):
-        return joined + is_open(win, 0, head) * is_open(win, 1, head) * is_open(win, 2, head)
-
-    split = jnp.where(lax.fori_loop(0, HEADS, count, jnp.int32(0)) <= WHOLE, 1, 0)
+    joined = jnp.int32(0)
+    for head in range(HEADS):
+        joined = joined + is_open(win, 0, head) * is_open(win, 1, head) * is_open(win, 2, head)
+    split = jnp.where(joined <= WHOLE, 1, 0)
 
     def told(head, wide, at, frames, heights):
         half = jnp.where(frames > heights, row, frame)
@@ -175,7 +172,7 @@
     @pl.when(facts[JOINED] > 0)
     def _():
         every = [pl.ds(0, 4 * TILE)]
-        chains([pl.ds(512 * block, 512) for block in range(3)], [every] * 3)
+        chains([pl.ds(TILE * block, TILE) for block in range(4)], [every] * 4)
 
     for index in range(2):
         here = (facts[LO] <= index) & (index < facts[HI])
@@ -210,8 +207,11 @@
         visit(qkv.at[:, 2 * DIM :], qkv, facts, None, keep(peak, total))
 
 
-def cut(facts, qkv, half, rest):
+def cut_rest(facts, qkv, rest):
     rest[...] = qkv[2 * TILE :, : 2 * DIM]
+
+
+def cut(facts, qkv, half):
     half[:TILE, :] = qkv[tile_rows(facts[FIRST]), : 2 * DIM]
     half[TILE:, :] = qkv[tile_rows(facts[SECOND]), : 2 * DIM]
 
@@ -354,7 +354,7 @@
 
     lower, upper = beside(qkv[:, : 2 * DIM], 0)
     pair = jax.ShapeDtypeStruct((rows // 2, 2 * DIM), bf16)
-    half, rest = call(cut, (pair, pair), [facts, qkv])
+    half = call(cut, pair, [facts, qkv])
     low_half, up_half = beside(half, 1)
 
     column = lax.axis_index("col")
@@ -371,7 +371,9 @@
     def no_rest(rest):
         return (jnp.zeros_like(rest),) * 2
 
-    low_rest, up_rest = lax.cond(whole, send_rest, no_rest, rest)
+    low_rest, up_rest = lax.cond(
+        whole, send_rest, no_rest, call(cut_rest, pair, [facts, qkv])
+    )
 
     state = (jax.ShapeDtypeStruct((rows, DIM), f32), jax.ShapeDtypeStruct((rows, 2 * DIM), f32))
 

time: 75.2 us -> 75.1 us (level)
  the two profiles are of different devices: /device:TPU:417 before, /device:TPU:353 now
where the time goes in v2:
time: 75.1 us; the launch traced here: 74.8 us
  blocking collectives  30.6 us (41%)
  waiting for transfers between devices  15.7 us (21%)
  starting transfers between devices  12.4 us (17%)
  Pallas kernels  11.9 us (16%)
  local copies, waits for them, and re-layouts  2.49 us (3%)
  between operations  0.96 us (1%)
    all_to_all x1, blocking collectives, exchange(): return lax.all_to_all(value, GROUP, split_axis=0, concat_axis=0, tiled=True)  30.6 us
    all_to_all x1, waiting for transfers between devices, exchange(): return lax.all_to_all(value, GROUP, split_axis=0, concat_axis=0, tiled=True)  15.7 us
    all_to_all x1, starting transfers between devices, exchange(): return lax.all_to_all(value, GROUP, split_axis=0, concat_axis=0, tiled=True)  8.9 us
    pallas_call x5, Pallas kernels, call(): pl.pallas_call(kernel, out_shape=shapes, in_specs=[SMEM] + [VMEM] * (len(...  6.67 us
    pallas_call x1, Pallas kernels, shards(): pl.pallas_call(pack_kernel, out_shape=jax.ShapeDtypeStruct((MEMBERS, toke...  2.28 us
    ppermute x2, starting transfers between devices, beside(): lax.ppermute(value, along, up)  2.13 us
    pallas_call x1, Pallas kernels, shards(): pl.pallas_call(facts_kernel, out_shape=jax.ShapeDtypeStruct((HEAD + HEADS...  1.61 us
    another operation x2, local copies, waits for them, and re-layouts  1.54 us
  transfers between devices with their start and end apart: 5, of which 1 were waited for; matrix products, arithmetic and copies ran while one was open for 3% of the time, Pallas kernels for 10%

profile of v2, /device:TPU:353, one launch (start us, length us, event | category | flops | bytes accessed | tf_op | source)
XLA Modules:
  0.0 74.8 jit_solution(10555691666735778343)
XLA Ops:
  0.0 0.0 copy-start
  0.0 2.3 %shard_map.46 = bf16[32,48,384]{2,1,0:T(8,128)(2,1)} custom-call(s32[3,24]{1,0:T(4,128)} %bitcast.18, bf16[48,3072]{1,0:T(8,128)(2,1)} %refs_1_.1, bf16[48,3072]{1,0:T(8,128)(2,1)} %refs_2_.1, bf16[48,3072]{1,0:T(8,128)(2,1)} %refs_3_.1), custom_call_target="tpu_custom_call" | custom-call | tf_op jit(solution)/shard_map/pallas_call | solution.py:313
  2.3 8.9 %all-to-all-start.1 = ((bf16[32,48,384]{2,1,0:T(8,128)(2,1)}), bf16[32,48,384]{2,1,0:T(8,128)(2,1)S(1)}, u32[]{:S(2)}, u32[]{:S(2)}) async-start(bf16[32,48,384]{2,1,0:T(8,128)(2,1)} %shard_map.46), calls=%async_computation.1 | async-start | bytes 2359296 | tf_op jit(solution)/shard_map/all_to_all | solution.py:311
  11.2 0.1 pad_add_fusion.refs_1_
  11.3 0.0 copy-done
  11.3 1.6 %shard_map.47.facts = s32[36]{0:T(128)S(1)} custom-call(s32[3,24]{1,0:T(4,128)S(1)} %bitcast.19, s32[4]{0:T(128)S(1)} %pad_add_fusion.refs_1_), custom_call_target="tpu_custom_call" | custom-call | tf_op jit(solution)/shard_map/pallas_call | solution.py:333
  12.9 0.6 reduce_sum.9
  14.2 15.7 %all-to-all-done.1 = bf16[32,48,384]{2,1,0:T(8,128)(2,1)S(1)} async-done(((bf16[32,48,384]{2,1,0:T(8,128)(2,1)}), bf16[32,48,384]{2,1,0:T(8,128)(2,1)S(1)}, u32[]{:S(2)}, u32[]{:S(2)}) %all-to-all-start.1) | async-done | bytes 1179680 | tf_op jit(solution)/shard_map/all_to_all | solution.py:311
  29.9 1.0 %slice.4 = bf16[1536,256]{1,0:T(8,128)(2,1)} slice(bf16[1536,384]{1,0:T(8,128)(2,1)S(1)} %bitcast.11), slice={[0:1536], [0:256]} | slice | bytes 1572864 | tf_op jit(solution)/shard_map/slice | solution.py:355
  30.9 0.7 collective-permute-start.2
  31.6 0.7 collective-permute-start
  32.3 0.6 shard_map.48
  32.9 1.4 %collective-permute-start.3 = (bf16[768,256]{1,0:T(8,128)(2,1)S(1)}, bf16[768,256]{1,0:T(8,128)(2,1)}, u32[]{:S(2)}, u32[]{:S(2)}) collective-permute-start(bf16[768,256]{1,0:T(8,128)(2,1)S(1)} %shard_map.48), channel_id=1, source_target_pairs={{4,12},{12,20},{20,28},{28,36},{36,44},{44,52},{52,60},{68,76},{76... | collective-permute-start | bytes 1179656 | tf_op jit(solution)/shard_map/ppermute | solution.py:353
  34.3 0.7 collective-permute-start.1
  35.0 1.3 %shard_map.49 = bf16[768,256]{1,0:T(8,128)(2,1)} custom-call(s32[36]{0:T(128)S(1)} %shard_map.47.facts, bf16[1536,384]{1,0:T(8,128)(2,1)S(1)} %bitcast.13), custom_call_target="tpu_custom_call" | custom-call | tf_op jit(solution)/shard_map/pallas_call | solution.py:284
  36.3 1.5 %conditional.1 = (bf16[768,256]{1,0:T(8,128)(2,1)}, bf16[768,256]{1,0:T(8,128)(2,1)}) conditional(s32[]{:T(128)} %convert_element_type.3, () %tuple.15, (s32[]{:T(128)}, bf16[768,256]{1,0:T(8,128)(2,1)}) %tuple.16), branch_computations={%region_2.3_spmd, %region_3.4_spmd} | conditional | flops 1572894 | bytes 14549140 | solution.py:374
  36.3 0.8 %broadcast.24.clone = bf16[768,256]{1,0:T(8,128)(2,1)} broadcast(bf16[]{:T(256)} %constant.41.clone), dimensions={} | broadcast | bytes 393218 | tf_op jit(solution)/shard_map/broadcast.1
  37.1 0.8 %broadcast.24 = bf16[768,256]{1,0:T(8,128)(2,1)} broadcast(bf16[]{:T(256)} %constant.41.clone), dimensions={} | broadcast | bytes 393218 | tf_op jit(solution)/shard_map/broadcast.1
  37.9 2.7 %shard_map.50 = (f32[1536,128]{1,0:T(8,128)S(1)}, f32[1536,256]{1,0:T(8,128)S(1)}) custom-call(s32[36]{0:T(128)S(1)} %shard_map.47.facts, bf16[1536,384]{1,0:T(8,128)(2,1)S(1)} %bitcast.14, bf16[768,256]{1,0:T(8,128)(2,1)} %get-tuple-element.23.low_rest.rest, bf16[768,256]{1,0:T(8,128)(2,1)} %get-tuple-element.24.up_rest.rest), custom_call_target="tpu_custom_call" | custom-call | tf_op jit(solution)/shard_map/pallas_call | solution.py:284
  40.6 0.0 collective-permute-done.3.half
  40.6 0.0 collective-permute-done.2.every
  40.6 1.4 %shard_map.51 = (f32[1536,128]{1,0:T(8,128)S(1)}, f32[1536,256]{1,0:T(8,128)S(1)}) custom-call(s32[36]{0:T(128)S(1)} %shard_map.47.facts, bf16[1536,384]{1,0:T(8,128)(2,1)S(1)} %bitcast.15, bf16[1536,256]{1,0:T(8,128)(2,1)S(1)} %collective-permute-done.2.every, bf16[768,256]{1,0:T(8,128)(2,1)} %collective-permute-done.3.half, ...), custom_call_target="tpu_custom_call" | custom-call | tf_op jit(solution)/shard_map/pallas_call | solution.py:284
  42.0 0.0 collective-permute-done.1.half
  42.0 0.0 collective-permute-done.every
  42.0 0.7 shard_map.52
  42.7 30.6 %all_to_all.14.received = bf16[32,48,128]{2,1,0:T(8,128)(2,1)S(1)} all-to-all(bf16[32,48,128]{2,1,0:T(8,128)(2,1)S(1)} %bitcast.17), channel_id=1, replica_groups=mesh['uly'=8,'col'=8,'f'=2,'g'=2,'cfg'=2] {'f','g','uly'}, dimensions={0} | all-to-all | bytes 786432 | tf_op jit(solution)/shard_map/all_to_all | solution.py:311
  73.3 1.3 %shard_map.53 = bf16[48,3072]{1,0:T(8,128)(2,1)} custom-call(s32[36]{0:T(128)S(1)} %shard_map.47.facts, bf16[32,48,128]{2,1,0:T(8,128)(2,1)S(1)} %all_to_all.14.received), custom_call_target="tpu_custom_call" | custom-call | tf_op jit(solution)/shard_map/pallas_call | solution.py:397
  (1 shorter events, 0.0 us)
Async XLA Ops:
  0.0 11.3 %copy-start = (s32[24,3]{0,1:T(4,128)S(1)}, s32[24,3]{0,1:T(4,128)}, u32[]{:S(2)}) copy-start(s32[24,3]{0,1:T(4,128)} %param.9) | copy-start | bytes 868
  2.3 27.7 %all-to-all-start.1 = ((bf16[32,48,384]{2,1,0:T(8,128)(2,1)}), bf16[32,48,384]{2,1,0:T(8,128)(2,1)S(1)}, u32[]{:S(2)}, u32[]{:S(2)}) async-start(bf16[32,48,384]{2,1,0:T(8,128)(2,1)} %shard_map.46), calls=%async_computation.1 | async-start | bytes 2359296 | tf_op jit(solution)/shard_map/all_to_all | solution.py:311
  30.9 9.7 %collective-permute-start.2 = (bf16[1536,256]{1,0:T(8,128)(2,1)}, bf16[1536,256]{1,0:T(8,128)(2,1)S(1)}, u32[]{:S(2)}, u32[]{:S(2)}) collective-permute-start(bf16[1536,256]{1,0:T(8,128)(2,1)} %slice.4), channel_id=1, source_target_pairs={{8,0},{16,8},{24,16},{32,24},{40,32},{48,40},{56,48},{72,64},{80,7... | collective-permute-start | bytes 2359304 | tf_op jit(solution)/shard_map/ppermute | solution.py:353
  31.6 10.4 %collective-permute-start = (bf16[1536,256]{1,0:T(8,128)(2,1)}, bf16[1536,256]{1,0:T(8,128)(2,1)S(1)}, u32[]{:S(2)}, u32[]{:S(2)}) collective-permute-start(bf16[1536,256]{1,0:T(8,128)(2,1)} %slice.4), channel_id=1, source_target_pairs={{0,8},{8,16},{16,24},{24,32},{32,40},{40,48},{48,56},{64,72},{72,8... | collective-permute-start | bytes 2359304 | tf_op jit(solution)/shard_map/ppermute | solution.py:353
  32.9 7.7 %collective-permute-start.3 = (bf16[768,256]{1,0:T(8,128)(2,1)S(1)}, bf16[768,256]{1,0:T(8,128)(2,1)}, u32[]{:S(2)}, u32[]{:S(2)}) collective-permute-start(bf16[768,256]{1,0:T(8,128)(2,1)S(1)} %shard_map.48), channel_id=1, source_target_pairs={{4,12},{12,20},{20,28},{28,36},{36,44},{44,52},{52,60},{68,76},{76... | collective-permute-start | bytes 1179656 | tf_op jit(solution)/shard_map/ppermute | solution.py:353
  34.3 7.7 %collective-permute-start.1 = (bf16[768,256]{1,0:T(8,128)(2,1)S(1)}, bf16[768,256]{1,0:T(8,128)(2,1)S(1)}, u32[]{:S(2)}, u32[]{:S(2)}) collective-permute-start(bf16[768,256]{1,0:T(8,128)(2,1)S(1)} %shard_map.48), channel_id=1, source_target_pairs={{12,4},{20,12},{28,20},{36,28},{44,36},{52,44},{60,52},{76,68},{84... | collective-permute-start | bytes 1179656 | tf_op jit(solution)/shard_map/ppermute | solution.py:353

commit v3 on v2

--- a/solution.py
+++ b/solution.py
@@ -20,7 +20,7 @@
 PACK_VMEM = 62 * 1024 * 1024
 GROUP = ("f", "g", "uly")
 EXP2_SCALE = DIM**-0.5 * 1.4426950408889634
-PARAMS = pltpu.CompilerParams(vmem_limit_bytes=20 * 1024 * 1024)
+PARAMS = pltpu.CompilerParams(vmem_limit_bytes=12 * 1024 * 1024)
 
 
 def is_open(win, axis, head):

time: 75.1 us -> 75.1 us (level)
  no operation moved by 1% of the time
where the time goes in v3:
time: 75.1 us; the launch traced here: 74.8 us
  blocking collectives  30.6 us (41%)
  waiting for transfers between devices  15.7 us (21%)
  starting transfers between devices  12.4 us (17%)
  Pallas kernels  11.9 us (16%)
  local copies, waits for them, and re-layouts  2.49 us (3%)
  between operations  0.96 us (1%)
    all_to_all x1, blocking collectives, exchange(): return lax.all_to_all(value, GROUP, split_axis=0, concat_axis=0, tiled=True)  30.6 us
    all_to_all x1, waiting for transfers between devices, exchange(): return lax.all_to_all(value, GROUP, split_axis=0, concat_axis=0, tiled=True)  15.7 us
    all_to_all x1, starting transfers between devices, exchange(): return lax.all_to_all(value, GROUP, split_axis=0, concat_axis=0, tiled=True)  8.9 us
    pallas_call x5, Pallas kernels, call(): pl.pallas_call(kernel, out_shape=shapes, in_specs=[SMEM] + [VMEM] * (len(...  6.67 us
    pallas_call x1, Pallas kernels, shards(): pl.pallas_call(pack_kernel, out_shape=jax.ShapeDtypeStruct((MEMBERS, toke...  2.28 us
    ppermute x2, starting transfers between devices, beside(): lax.ppermute(value, along, up)  2.13 us
    pallas_call x1, Pallas kernels, shards(): pl.pallas_call(facts_kernel, out_shape=jax.ShapeDtypeStruct((HEAD + HEADS...  1.61 us
    another operation x2, local copies, waits for them, and re-layouts  1.54 us
  transfers between devices with their start and end apart: 5, of which 1 were waited for; matrix products, arithmetic and copies ran while one was open for 3% of the time, Pallas kernels for 10%

profile of v3, /device:TPU:353, one launch (start us, length us, event | category | flops | bytes accessed | tf_op | source)
XLA Modules:
  0.0 74.8 jit_solution(13481953009924873124)
XLA Ops:
  0.0 0.0 copy-start
  0.0 2.3 %shard_map.46 = bf16[32,48,384]{2,1,0:T(8,128)(2,1)} custom-call(s32[3,24]{1,0:T(4,128)} %bitcast.18, bf16[48,3072]{1,0:T(8,128)(2,1)} %refs_1_.1, bf16[48,3072]{1,0:T(8,128)(2,1)} %refs_2_.1, bf16[48,3072]{1,0:T(8,128)(2,1)} %refs_3_.1), custom_call_target="tpu_custom_call" | custom-call | tf_op jit(solution)/shard_map/pallas_call | solution.py:313
  2.3 8.9 %all-to-all-start.1 = ((bf16[32,48,384]{2,1,0:T(8,128)(2,1)}), bf16[32,48,384]{2,1,0:T(8,128)(2,1)S(1)}, u32[]{:S(2)}, u32[]{:S(2)}) async-start(bf16[32,48,384]{2,1,0:T(8,128)(2,1)} %shard_map.46), calls=%async_computation.1 | async-start | bytes 2359296 | tf_op jit(solution)/shard_map/all_to_all | solution.py:311
  11.2 0.1 pad_add_fusion.refs_1_
  11.3 0.0 copy-done
  11.3 1.6 %shard_map.47.facts = s32[36]{0:T(128)S(1)} custom-call(s32[3,24]{1,0:T(4,128)S(1)} %bitcast.19, s32[4]{0:T(128)S(1)} %pad_add_fusion.refs_1_), custom_call_target="tpu_custom_call" | custom-call | tf_op jit(solution)/shard_map/pallas_call | solution.py:333
  12.9 0.6 reduce_sum.9
  14.2 15.7 %all-to-all-done.1 = bf16[32,48,384]{2,1,0:T(8,128)(2,1)S(1)} async-done(((bf16[32,48,384]{2,1,0:T(8,128)(2,1)}), bf16[32,48,384]{2,1,0:T(8,128)(2,1)S(1)}, u32[]{:S(2)}, u32[]{:S(2)}) %all-to-all-start.1) | async-done | bytes 1179680 | tf_op jit(solution)/shard_map/all_to_all | solution.py:311
  29.9 1.0 %slice.4 = bf16[1536,256]{1,0:T(8,128)(2,1)} slice(bf16[1536,384]{1,0:T(8,128)(2,1)S(1)} %bitcast.11), slice={[0:1536], [0:256]} | slice | bytes 1572864 | tf_op jit(solution)/shard_map/slice | solution.py:355
  30.9 0.7 collective-permute-start.2
  31.6 0.7 collective-permute-start
  32.3 0.6 shard_map.48
  32.9 1.4 %collective-permute-start.3 = (bf16[768,256]{1,0:T(8,128)(2,1)S(1)}, bf16[768,256]{1,0:T(8,128)(2,1)}, u32[]{:S(2)}, u32[]{:S(2)}) collective-permute-start(bf16[768,256]{1,0:T(8,128)(2,1)S(1)} %shard_map.48), channel_id=1, source_target_pairs={{4,12},{12,20},{20,28},{28,36},{36,44},{44,52},{52,60},{68,76},{76... | collective-permute-start | bytes 1179656 | tf_op jit(solution)/shard_map/ppermute | solution.py:353
  34.3 0.7 collective-permute-start.1
  35.0 1.3 %shard_map.49 = bf16[768,256]{1,0:T(8,128)(2,1)} custom-call(s32[36]{0:T(128)S(1)} %shard_map.47.facts, bf16[1536,384]{1,0:T(8,128)(2,1)S(1)} %bitcast.13), custom_call_target="tpu_custom_call" | custom-call | tf_op jit(solution)/shard_map/pallas_call | solution.py:284
  36.3 1.5 %conditional.1 = (bf16[768,256]{1,0:T(8,128)(2,1)}, bf16[768,256]{1,0:T(8,128)(2,1)}) conditional(s32[]{:T(128)} %convert_element_type.3, () %tuple.15, (s32[]{:T(128)}, bf16[768,256]{1,0:T(8,128)(2,1)}) %tuple.16), branch_computations={%region_2.3_spmd, %region_3.4_spmd} | conditional | flops 1572894 | bytes 14549140 | solution.py:374
  36.3 0.8 %broadcast.24.clone = bf16[768,256]{1,0:T(8,128)(2,1)} broadcast(bf16[]{:T(256)} %constant.41.clone), dimensions={} | broadcast | bytes 393218 | tf_op jit(solution)/shard_map/broadcast.1
  37.1 0.8 %broadcast.24 = bf16[768,256]{1,0:T(8,128)(2,1)} broadcast(bf16[]{:T(256)} %constant.41.clone), dimensions={} | broadcast | bytes 393218 | tf_op jit(solution)/shard_map/broadcast.1
  37.9 2.7 %shard_map.50 = (f32[1536,128]{1,0:T(8,128)S(1)}, f32[1536,256]{1,0:T(8,128)S(1)}) custom-call(s32[36]{0:T(128)S(1)} %shard_map.47.facts, bf16[1536,384]{1,0:T(8,128)(2,1)S(1)} %bitcast.14, bf16[768,256]{1,0:T(8,128)(2,1)} %get-tuple-element.23.low_rest.rest, bf16[768,256]{1,0:T(8,128)(2,1)} %get-tuple-element.24.up_rest.rest), custom_call_target="tpu_custom_call" | custom-call | tf_op jit(solution)/shard_map/pallas_call | solution.py:284
  40.6 0.0 collective-permute-done.3.half
  40.6 0.0 collective-permute-done.2.every
  40.6 1.4 %shard_map.51 = (f32[1536,128]{1,0:T(8,128)S(1)}, f32[1536,256]{1,0:T(8,128)S(1)}) custom-call(s32[36]{0:T(128)S(1)} %shard_map.47.facts, bf16[1536,384]{1,0:T(8,128)(2,1)S(1)} %bitcast.15, bf16[1536,256]{1,0:T(8,128)(2,1)S(1)} %collective-permute-done.2.every, bf16[768,256]{1,0:T(8,128)(2,1)} %collective-permute-done.3.half, ...), custom_call_target="tpu_custom_call" | custom-call | tf_op jit(solution)/shard_map/pallas_call | solution.py:284
  42.0 0.0 collective-permute-done.1.half
  42.0 0.0 collective-permute-done.every
  42.0 0.7 shard_map.52
  42.7 30.6 %all_to_all.14.received = bf16[32,48,128]{2,1,0:T(8,128)(2,1)S(1)} all-to-all(bf16[32,48,128]{2,1,0:T(8,128)(2,1)S(1)} %bitcast.17), channel_id=1, replica_groups=mesh['uly'=8,'col'=8,'f'=2,'g'=2,'cfg'=2] {'f','g','uly'}, dimensions={0} | all-to-all | bytes 786432 | tf_op jit(solution)/shard_map/all_to_all | solution.py:311
  73.3 1.3 %shard_map.53 = bf16[48,3072]{1,0:T(8,128)(2,1)} custom-call(s32[36]{0:T(128)S(1)} %shard_map.47.facts, bf16[32,48,128]{2,1,0:T(8,128)(2,1)S(1)} %all_to_all.14.received), custom_call_target="tpu_custom_call" | custom-call | tf_op jit(solution)/shard_map/pallas_call | solution.py:397
  (1 shorter events, 0.0 us)
Async XLA Ops:
  0.0 11.3 %copy-start = (s32[24,3]{0,1:T(4,128)S(1)}, s32[24,3]{0,1:T(4,128)}, u32[]{:S(2)}) copy-start(s32[24,3]{0,1:T(4,128)} %param.9) | copy-start | bytes 868
  2.3 27.7 %all-to-all-start.1 = ((bf16[32,48,384]{2,1,0:T(8,128)(2,1)}), bf16[32,48,384]{2,1,0:T(8,128)(2,1)S(1)}, u32[]{:S(2)}, u32[]{:S(2)}) async-start(bf16[32,48,384]{2,1,0:T(8,128)(2,1)} %shard_map.46), calls=%async_computation.1 | async-start | bytes 2359296 | tf_op jit(solution)/shard_map/all_to_all | solution.py:311
  30.9 9.7 %collective-permute-start.2 = (bf16[1536,256]{1,0:T(8,128)(2,1)}, bf16[1536,256]{1,0:T(8,128)(2,1)S(1)}, u32[]{:S(2)}, u32[]{:S(2)}) collective-permute-start(bf16[1536,256]{1,0:T(8,128)(2,1)} %slice.4), channel_id=1, source_target_pairs={{8,0},{16,8},{24,16},{32,24},{40,32},{48,40},{56,48},{72,64},{80,7... | collective-permute-start | bytes 2359304 | tf_op jit(solution)/shard_map/ppermute | solution.py:353
  31.6 10.4 %collective-permute-start = (bf16[1536,256]{1,0:T(8,128)(2,1)}, bf16[1536,256]{1,0:T(8,128)(2,1)S(1)}, u32[]{:S(2)}, u32[]{:S(2)}) collective-permute-start(bf16[1536,256]{1,0:T(8,128)(2,1)} %slice.4), channel_id=1, source_target_pairs={{0,8},{8,16},{16,24},{24,32},{32,40},{40,48},{48,56},{64,72},{72,8... | collective-permute-start | bytes 2359304 | tf_op jit(solution)/shard_map/ppermute | solution.py:353
  32.9 7.7 %collective-permute-start.3 = (bf16[768,256]{1,0:T(8,128)(2,1)S(1)}, bf16[768,256]{1,0:T(8,128)(2,1)}, u32[]{:S(2)}, u32[]{:S(2)}) collective-permute-start(bf16[768,256]{1,0:T(8,128)(2,1)S(1)} %shard_map.48), channel_id=1, source_target_pairs={{4,12},{12,20},{20,28},{28,36},{36,44},{44,52},{52,60},{68,76},{76... | collective-permute-start | bytes 1179656 | tf_op jit(solution)/shard_map/ppermute | solution.py:353
  34.3 7.7 %collective-permute-start.1 = (bf16[768,256]{1,0:T(8,128)(2,1)S(1)}, bf16[768,256]{1,0:T(8,128)(2,1)S(1)}, u32[]{:S(2)}, u32[]{:S(2)}) collective-permute-start(bf16[768,256]{1,0:T(8,128)(2,1)S(1)} %shard_map.48), channel_id=1, source_target_pairs={{12,4},{20,12},{28,20},{36,28},{44,36},{52,44},{60,52},{76,68},{84... | collective-permute-start | bytes 1179656 | tf_op jit(solution)/shard_map/ppermute | solution.py:353
